TPU v7x, 32 devices: a whole 2x2x4 slice. The times are simulated.
32 devices in a mesh: mp: 2 (over x), row: 4 (over z), col: 4 (over y, core).
Axes of the slice: x: 2, y: 2, z: 4, core: 2. Of those that a mesh axis runs over, the one named last changes fastest.
Arguments:
- gram_tiles: bfloat16 [4, 4, 4, 1024, 16384], P('mp', None, 'row', None, 'col'), may hold values from -4 to 64, as said below
- weights: bfloat16 [4, 16384, 128], P('mp', ('col', 'row')), may hold values from -8 to 8
- damping: float32 [128], replicated, may hold values from 0.5 to 4
Outputs:
- merged: float32 [16384, 128], P(('col', 'row'))
- residual: float32 [16384, 128], P(('col', 'row'))
Inputs may be any that keep to these rules, and one draw needn't show every extreme that they name: `gram_tiles`: each model's 16384 x 16384 Gram, read as in the first step, is symmetric positive definite.
All inputs are finite; a program needn't handle non-finite values.
Results may differ from a plain program's by a relative error of at most 0.012.
The roundings to bfloat16 on the way count: a program that leaves them out, or rounds other values in their place, can miss the bound.
Values may be sent and summed in bfloat16 or wider, within the bound.
A program may use at most 128 MiB of HBM per device.

v0:
```python
import jax
import jax.numpy as jnp
from jax import lax
from jax.sharding import PartitionSpec as P

ITERS = 2


def contract_rows(gram_tile, portion):
    spread = jnp.broadcast_to(portion, (gram_tile.shape[0],) + portion.shape[1:])
    return jnp.einsum("mij,mjk->ik", gram_tile, spread, preferred_element_type=jnp.float32)


def apply_models(gram_tile, vectors):
    partial_value = contract_rows(gram_tile, lax.all_gather(vectors, "row", axis=1, tiled=True))
    summed = lax.psum_scatter(partial_value, "col", scatter_dimension=0, tiled=True)
    return (lax.psum(summed, "mp"), partial_value)


def squares(residual):
    return lax.psum(jnp.sum(residual * residual, axis=0), ("row", "col"))


def on_device(gram_tiles, weights, damping):
    shape_in = gram_tiles.shape
    gram_tile = gram_tiles.reshape(
        shape_in[0], shape_in[1] * shape_in[2] * shape_in[3], shape_in[4]
    )
    target, unused = apply_models(gram_tile, weights)
    merged = jnp.zeros_like(target)
    residual = target
    direction = target
    norm_now = squares(residual)
    for iteration in range(ITERS):
        low_dir = direction.astype(jnp.bfloat16)
        applied, partial_value = apply_models(gram_tile, low_dir[None])
        dir_wide = low_dir.astype(jnp.float32)
        applied = applied + damping[None, :] * dir_wide
        curve_term = lax.psum(jnp.sum(dir_wide * applied, axis=0), ("row", "col"))
        step_size = norm_now / curve_term
        merged = merged + step_size[None, :] * direction
        residual = residual - step_size[None, :] * applied
        if iteration + 1 < ITERS:
            norm_next = squares(residual)
            direction = residual + (norm_next / norm_now)[None, :] * direction
            norm_now = norm_next
    return (merged, residual)


def solution(mesh):
    in_specs = (P("mp", None, "row", None, "col"), P("mp", ("col", "row"), None), P())
    out_specs = (P(("col", "row"), None), P(("col", "row"), None))
    return jax.shard_map(
        on_device, mesh=mesh, in_specs=in_specs, out_specs=out_specs, check_vma=False
    )
```

profile of v0, /device:TPU:0, one launch (start us, length us, event | category | flops | bytes accessed | tf_op | source)
XLA Modules:
  0.0 491.7 jit_solution(9483522658742069603)
XLA Ops:
  7.2 0.7 all-gather.6.cloned.1.call-update
  7.9 0.0 reduce-scatter.4.cloned.1.call-start
  7.9 50.3 %all-gather.6.cloned.1.call-done = bf16[2,4096,128]{2,1,0:T(8,128)(2,1)} async-done(((bf16[2,1024,128]{2,1,0:T(8,128)(2,1)}), bf16[2,4096,128]{2,1,0:T(8,128)(2,1)}) %all-gather.6.cloned.1.call-update) | async-done | bytes 2097168 | tf_op jit(solution)/shard_map/all_gather | solution.py:15
  58.2 27.3 %convolution_bitcast_fusion.2 = f32[4096,128]{1,0:T(8,128)} fusion(bf16[2,4096,4096]{2,1,0:T(8,128)(2,1)} %bitcast, bf16[2,4096,128]{2,1,0:T(8,128)(2,1)} %all-gather.6.cloned.1.call-done), kind=kOutput, calls=%fused_computation.2 | convolution fusion | flops 8589934592 | bytes 71303168 | tf_op jit(solution)/shard_map/mij,mjk->ik/dot_general | solution.py:11
  85.6 0.0 all-reduce.5.cloned.1.call-start
  85.6 30.3 %reduce-scatter.4.cloned.1.call-done = f32[1024,128]{1,0:T(8,128)} async-done(((f32[4096,128]{1,0:T(8,128)}), f32[1024,128]{1,0:T(8,128)}) %reduce-scatter.4.cloned.1.call-update) | async-done | bytes 524304 | tf_op jit(solution)/shard_map/reduce_scatter | solution.py:16
  115.9 0.0 all-gather.8.cloned.1.call-start
  116.0 30.9 %all-reduce.5.cloned.1.call-done = f32[1024,128]{1,0:T(8,128)} async-done(((f32[1024,128]{1,0:T(8,128)}), f32[1024,128]{1,0:T(8,128)}) %all-reduce.5.cloned.1.call-update) | async-done | bytes 524304 | tf_op jit(solution)/shard_map/psum | solution.py:17
  146.9 1.8 convert_element_type.12
  148.7 0.0 reduce-scatter.6.cloned.1.call-start
  148.8 28.1 %all-gather.8.cloned.1.call-done = bf16[4096,128]{1,0:T(8,128)(2,1)} async-done(((bf16[1024,128]{1,0:T(8,128)(2,1)}), bf16[4096,128]{1,0:T(8,128)(2,1)}) %all-gather.8.cloned.1.call-update) | async-done | bytes 1048592 | tf_op jit(solution)/shard_map/all_gather | solution.py:15
  176.9 1.5 copy.5
  178.4 27.1 %convolution_bitcast_fusion.1 = f32[4096,128]{1,0:T(8,128)} fusion(bf16[2,4096,4096]{2,1,0:T(8,128)(2,1)} %bitcast, bf16[4096,128]{0,1:T(8,128)(2,1)S(1)} %copy.5), kind=kOutput, calls=%fused_computation.1 | convolution fusion | flops 8589934592 | bytes 70254592 | tf_op jit(solution)/shard_map/mij,mjk->ik/dot_general | solution.py:11
  205.5 0.0 all-reduce.7.cloned.1.call-start
  205.5 31.0 %reduce-scatter.6.cloned.1.call-done = f32[1024,128]{1,0:T(8,128)} async-done(((f32[4096,128]{1,0:T(8,128)}), f32[1024,128]{1,0:T(8,128)}) %reduce-scatter.6.cloned.1.call-update) | async-done | bytes 524304 | tf_op jit(solution)/shard_map/reduce_scatter | solution.py:16
  236.6 0.0 all-gather.10.cloned.1.call-start
  236.6 30.8 %all-reduce.7.cloned.1.call-done = f32[1024,128]{1,0:T(8,128)} async-done(((f32[1024,128]{1,0:T(8,128)}), f32[1024,128]{1,0:T(8,128)}) %all-reduce.7.cloned.1.call-update) | async-done | bytes 524304 | tf_op jit(solution)/shard_map/psum | solution.py:17
  267.5 1.3 fusion.3
  268.7 33.2 %all-reduce = (f32[128]{0:T(128)S(1)}, f32[128]{0:T(128)S(1)}) all-reduce(f32[128]{0:T(128)S(1)} %get-tuple-element.3, f32[128]{0:T(128)S(1)} %get-tuple-element.2), channel_id=1, replica_groups=mesh['mp'=2,'row'=4,'col'=4] {'row','col'}, use_global_device_ids=true, to_apply=%region_3.0 | all-reduce | flops 256 | bytes 2048 | tf_op jit(solution)/shard_map/psum | solution.py:21
  301.9 1.2 multiply_reduce_fusion
  303.1 29.5 %psum.53 = f32[128]{0:T(128)S(1)} all-reduce(f32[128]{0:T(128)S(1)} %multiply_reduce_fusion), channel_id=1, replica_groups=mesh['mp'=2,'row'=4,'col'=4] {'row','col'}, use_global_device_ids=true, to_apply=%region_9.0 | all-reduce | flops 128 | bytes 1024 | tf_op jit(solution)/shard_map/psum | solution.py:21
  332.6 0.8 fusion.6
  333.4 0.0 reduce-scatter.8.cloned.1.call-start
  333.5 24.4 %all-gather.10.cloned.1.call-done = bf16[4096,128]{1,0:T(8,128)(2,1)} async-done(((bf16[1024,128]{1,0:T(8,128)(2,1)}), bf16[4096,128]{1,0:T(8,128)(2,1)}) %all-gather.10.cloned.1.call-update) | async-done | bytes 1048592 | tf_op jit(solution)/shard_map/all_gather | solution.py:15
  357.8 1.5 copy.7
  359.3 27.1 %convolution_bitcast_fusion = f32[4096,128]{1,0:T(8,128)} fusion(bf16[2,4096,4096]{2,1,0:T(8,128)(2,1)} %bitcast, bf16[4096,128]{0,1:T(8,128)(2,1)S(1)} %copy.7), kind=kOutput, calls=%fused_computation | convolution fusion | flops 8589934592 | bytes 70254592 | tf_op jit(solution)/shard_map/mij,mjk->ik/dot_general | solution.py:11
  386.5 0.0 all-reduce.9.cloned.1.call-start
  386.5 31.0 %reduce-scatter.8.cloned.1.call-done = f32[1024,128]{1,0:T(8,128)} async-done(((f32[4096,128]{1,0:T(8,128)}), f32[1024,128]{1,0:T(8,128)}) %reduce-scatter.8.cloned.1.call-update) | async-done | bytes 524304 | tf_op jit(solution)/shard_map/reduce_scatter | solution.py:16
  417.5 31.0 %all-reduce.9.cloned.1.call-done = f32[1024,128]{1,0:T(8,128)} async-done(((f32[1024,128]{1,0:T(8,128)}), f32[1024,128]{1,0:T(8,128)}) %all-reduce.9.cloned.1.call-update) | async-done | bytes 524304 | tf_op jit(solution)/shard_map/psum | solution.py:17
  448.6 1.2 fusion.5
  449.7 33.2 %psum.55 = f32[128]{0:T(128)S(1)} all-reduce(f32[128]{0:T(128)S(1)} %fusion.5), channel_id=1, replica_groups=mesh['mp'=2,'row'=4,'col'=4] {'row','col'}, use_global_device_ids=true, to_apply=%region_13.0 | all-reduce | flops 128 | bytes 1024 | tf_op jit(solution)/shard_map/psum | solution.py:39
  482.9 2.3 multiply_subtract_fusion
  (20 shorter events, 0.2 us)
Async XLA Ops:
  7.2 51.1 %all-gather.6.cloned.1.call-start = ((), (), s32[]{:S(2)}) async-start(), calls=%async_computation.3 | async-start | bytes 2621440 | tf_op jit(solution)/shard_map/all_gather | solution.py:15
  7.9 108.0 %reduce-scatter.4.cloned.1.call-start = ((), (), s32[]{:S(2)}) async-start(), calls=%async_computation.4 | async-start | bytes 2621440 | tf_op jit(solution)/shard_map/reduce_scatter | solution.py:16
  85.6 61.3 %all-reduce.5.cloned.1.call-start = ((), (), s32[]{:S(2)}) async-start(), calls=%async_computation.5 | async-start | bytes 1048576 | tf_op jit(solution)/shard_map/psum | solution.py:17
  115.9 61.0 %all-gather.8.cloned.1.call-start = ((), (), s32[]{:S(2)}) async-start(), calls=%async_computation.10 | async-start | bytes 1310720 | tf_op jit(solution)/shard_map/all_gather | solution.py:15
  148.7 87.9 %reduce-scatter.6.cloned.1.call-start = ((), (), s32[]{:S(2)}) async-start(), calls=%async_computation.6 | async-start | bytes 2621440 | tf_op jit(solution)/shard_map/reduce_scatter | solution.py:16
  205.5 62.0 %copy-start = (f32[1024,128]{1,0:T(8,128)S(1)}, f32[1024,128]{1,0:T(8,128)}, u32[]{:S(2)}) copy-start(f32[1024,128]{1,0:T(8,128)} %all-reduce.5.cloned.1.call-done) | copy-start | bytes 1572868
  205.5 62.0 %copy-start.3 = (f32[128]{0:T(128)S(1)}, f32[128]{0:T(128)}, u32[]{:S(2)}) copy-start(f32[128]{0:T(128)} %param.5) | copy-start | bytes 1540
  205.5 61.9 %all-reduce.7.cloned.1.call-start = ((), (), s32[]{:S(2)}) async-start(), calls=%async_computation.7 | async-start | bytes 1048576 | tf_op jit(solution)/shard_map/psum | solution.py:17
  236.6 121.3 %all-gather.10.cloned.1.call-start = ((), (), s32[]{:S(2)}) async-start(), calls=%async_computation.11 | async-start | bytes 1310720 | tf_op jit(solution)/shard_map/all_gather | solution.py:15
  267.4 65.1 %copy-start.1 = (f32[1024,128]{1,0:T(8,128)S(1)}, f32[1024,128]{1,0:T(8,128)}, u32[]{:S(2)}) copy-start(f32[1024,128]{1,0:T(8,128)} %all-reduce.7.cloned.1.call-done) | copy-start | bytes 1572868
  333.4 84.1 %reduce-scatter.8.cloned.1.call-start = ((), (), s32[]{:S(2)}) async-start(), calls=%async_computation.8 | async-start | bytes 2621440 | tf_op jit(solution)/shard_map/reduce_scatter | solution.py:16
  386.4 62.1 %copy-start.2 = (bf16[1024,128]{1,0:T(8,128)(2,1)S(1)}, bf16[1024,128]{1,0:T(8,128)(2,1)}, u32[]{:S(2)}) copy-start(bf16[1024,128]{1,0:T(8,128)(2,1)} %fusion.6) | copy-start | bytes 786436
  386.5 62.1 %all-reduce.9.cloned.1.call-start = ((), (), s32[]{:S(2)}) async-start(), calls=%async_computation.9 | async-start | bytes 1048576 | tf_op jit(solution)/shard_map/psum | solution.py:17
Sparse Core Ops, SparseCore 0:
  9.6 48.6 all-gather.5
  85.7 30.1 reduce-scatter.3
  118.3 28.5 all-reduce.4
  148.9 27.9 all-gather.7
  205.6 30.9 reduce-scatter.5
  238.8 28.5 all-reduce.6
  333.6 24.2 all-gather.9
  386.6 30.9 reduce-scatter.7
  419.9 28.5 all-reduce.8
where the time goes:
time: 492 us
  waiting for transfers between devices  289 us (59%)
  blocking collectives  95.8 us (19%)
  matrix products  81.5 us (17%)
  between operations  13.9 us (3%)
  other arithmetic  8.54 us (2%)
    all_gather x3, waiting for transfers between devices, apply_models(): lax.all_gather(vectors, 'row', axis=1, tiled=True)  103 us
    psum x3, waiting for transfers between devices, apply_models(): return (lax.psum(summed, 'mp'), partial_value)  92.7 us
    reduce_scatter x3, waiting for transfers between devices, apply_models(): lax.psum_scatter(partial_value, 'col', scatter_dimension=0, tiled=True)  92.3 us
    dot_general x3, matrix products, contract_rows(): jnp.einsum('mij,mjk->ik', gram_tile, spread, preferred_element_type=jnp.f...  81.5 us
    psum x2, blocking collectives, squares(): return lax.psum(jnp.sum(residual * residual, axis=0), ('row', 'col'))  62.6 us
    psum x1, blocking collectives, on_device(): curve_term = lax.psum(jnp.sum(dir_wide * applied, axis=0), ('row', 'col'))  33.2 us
  transfers between devices with their start and end apart: 9, of which 9 were waited for; matrix products, arithmetic and copies ran while one was open for 0% of the time, Pallas kernels for 0%

commit v1 on v0

v1 whole, which is shorter than its diff:
```python
import functools

import jax
import jax.numpy as jnp
from jax import lax
from jax.experimental import pallas as pl
from jax.experimental.pallas import tpu as pltpu
from jax.sharding import PartitionSpec as P

ITERS = 2
NBUF = 8
MESH = pl.DeviceIdType.MESH
F32 = jnp.float32
BF16 = jnp.bfloat16


def kernel(n_mp, n_row, n_col, gram, w_ref, damp, merged, resid,
           gsum, stage, part, xg, lg, csend, crecv, ysend, yrecv, mwide, mbuf, diag, dirn, sc1, sc2,
           gsem, zs, zr, xs, xr, cs, cr, ys, yr, ms, mr, ds, dr, s1s, s1r, s2s, s2r):
    M, R, C = n_mp, n_row, n_col
    H = C // 2
    models, piece, width = w_ref.shape
    half = piece // M
    tile = min(piece, 256)
    parts = piece // tile
    mp, r, c = lax.axis_index("mp"), lax.axis_index("row"), lax.axis_index("col")
    h, core = c // 2, c % 2

    def at_row(k):
        return {"row": k}

    def at_col(k):
        return {"col": k}

    def at_mp(k):
        return {"mp": k}

    def remote(src, dst, send, recv, device):
        return pltpu.make_async_remote_copy(
            src_ref=src, dst_ref=dst, send_sem=send, recv_sem=recv,
            device_id=device, device_id_type=MESH)

    def piece_at(i):
        low = jnp.minimum(r, R - 1 - r)
        d = (i + 1) // 2
        both = jnp.where(i % 2 == 1, r - d, r + d)
        one = jnp.where(r < R - 1 - r, r + (i - low), r - (i - low))
        return jnp.where(i <= 2 * low, both, one)

    def col_at(k):
        group = (h + k // 2 + 1) % H
        return 2 * group + jnp.where(k % 2 == 0, 1 - core, core)

    def stream(u):
        t = u // parts
        p, cc = piece_at(t // C), col_at(t % C)
        slot = u % NBUF
        return pltpu.make_async_copy(
            gram.at[:, cc, rows_of(u % parts), pl.ds(pl.multiple_of(p * piece, piece), piece)],
            stage.at[slot], gsem.at[slot])

    def rows_of(j):
        return pl.ds(pl.multiple_of(j * tile, tile), tile)

    for u in range(min(NBUF - 1, R * C * parts)):
        stream(u).start()

    barrier = pltpu.get_barrier_semaphore()
    for k in range(1, C):
        pl.semaphore_signal(barrier, inc=1, device_id=at_col((c + k) % C), device_id_type=MESH)
    for k in range(1, R):
        pl.semaphore_signal(barrier, inc=1, device_id=at_row((r + k) % R), device_id_type=MESH)
    for k in range(1, M):
        pl.semaphore_signal(barrier, inc=1, device_id=at_mp((mp + k) % M), device_id_type=MESH)
    pl.semaphore_wait(barrier, C + R + M - 3)

    def zref(n, p):
        if n == 0:
            return xg.at[p]
        return lg.at[n - 1, p, pl.ds(pl.multiple_of(mp * half, half), half)]

    def zcopy(n, p, up):
        ref = zref(n, p)
        return remote(ref, ref, zs.at[n, up, p], zr.at[n, p], at_row(r + 1 if up else r - 1))

    def zsend(n, p, wait=False):
        @pl.when(jnp.logical_and(p <= r, r < R - 1))
        def _():
            copy = zcopy(n, p, 1)
            copy.wait_send() if wait else copy.start()

        @pl.when(jnp.logical_and(p >= r, r > 0))
        def _():
            copy = zcopy(n, p, 0)
            copy.wait_send() if wait else copy.start()

    def zwait(n, p):
        ref = zref(n, p)
        remote(ref, ref, zs.at[n, 0, p], zr.at[n, p],
               at_row(jnp.where(p < r, r - 1, r + 1))).wait_recv()

    def xcopy(n, p, k):
        ref = lg.at[n - 1, p, pl.ds(pl.multiple_of(mp * half, half), half)]
        return remote(ref, ref, xs.at[n, k - 1, p], xr.at[n, k - 1, p], at_mp((mp + k) % M))

    def xwait(n, p, k):
        other = (mp + M - k) % M
        ref = lg.at[n - 1, p, pl.ds(pl.multiple_of(other * half, half), half)]
        remote(ref, ref, xs.at[n, k - 1, p], xr.at[n, k - 1, p], at_mp(other)).wait_recv()

    def first_block(t, p):
        cc = col_at(t % C)

        def body(j, carry):
            u = t * parts + j
            stream(u).wait()

            @pl.when(u + NBUF - 1 < R * C * parts)
            def _():
                stream(u + NBUF - 1).start()

            slot = u % NBUF
            rows = rows_of(j)
            value = part[cc, rows, :]
            total = None
            for m in range(models):
                g = stage[slot, m]
                value += jnp.dot(g, xg[p, m], preferred_element_type=F32)
                total = g if total is None else total + g
            part[cc, rows, :] = value
            gsum[cc, p, rows, :] = total

            if not isinstance(t, int) or t == C - 1:
                @pl.when(t == C - 1)
                def _():
                    split_diagonal(j, slot)

            return carry

        lax.fori_loop(0, parts, body, 0)

    def diag_copy(m, k, device):
        return remote(diag.at[m], diag.at[m], ds.at[k - 1], dr.at[k - 1], at_mp(device))

    def split_diagonal(j, slot):
        rows = rows_of(j)
        wide = None
        for m in range(models):
            g = stage[slot, m].astype(F32)
            wide = g if wide is None else wide + g
        row_ids = lax.broadcasted_iota(jnp.int32, (tile, piece), 0) + j * tile
        on = row_ids == lax.broadcasted_iota(jnp.int32, (tile, piece), 1)
        gsum[c, r, rows, :] = jnp.where(on, 0.0, wide).astype(BF16)
        column = jnp.sum(jnp.where(on, wide, 0.0), axis=1, keepdims=True)
        diag[mp, rows, :] = jnp.broadcast_to(column, (tile, width))

    def later_block(n, cc, p):
        def body(j, carry):
            rows = rows_of(j)
            part[cc, rows, :] += jnp.dot(
                gsum[cc, p, rows, :], lg[n - 1, p], preferred_element_type=F32)
            return carry

        lax.fori_loop(0, piece // tile, body, 0)

    def finish(n, block):
        def core_copy(s):
            return remote(csend.at[s], crecv.at[n, s], cs.at[n, s], cr.at[n, s], at_col(c + 1 - 2 * core))

        def y_copy(s):
            return remote(ysend.at[s], yrecv.at[n, s], ys.at[n, s], yr.at[n, s],
                          at_col(2 * ((h + s + 1) % H) + core))

        for s in range(H):
            group = (h + s + 1) % H
            theirs, mine = 2 * group + 1 - core, 2 * group + core
            block(2 * s, theirs)
            csend[s] = part[theirs].astype(BF16)
            core_copy(s).start()
            block(2 * s + 1, mine)
            core_copy(s).wait_recv()
            value = part[mine] + crecv[n, s].astype(F32)
            if s < H - 1:
                ysend[s] = value.astype(BF16)
                y_copy(s).start()
        for s in range(H - 1):
            y_copy(s).wait_recv()
            value += yrecv[n, s].astype(F32)
        held = mwide if n == 0 else mbuf.at[n - 1]

        def m_copy(m, k, device):
            return remote(held.at[m], held.at[m], ms.at[n, k - 1], mr.at[n, k - 1], at_mp(device))

        held[mp] = value.astype(held.dtype)
        for k in range(1, M):
            m_copy(mp, k, (mp + k) % M).start()
        for k in range(1, M):
            other = (mp + M - k) % M
            m_copy(other, k, other).wait_recv()
        total = held[0].astype(F32)
        for m in range(1, M):
            total += held[m].astype(F32)
        for s in range(H):
            core_copy(s).wait_send()
            if s < H - 1:
                y_copy(s).wait_send()
        for k in range(1, M):
            m_copy(mp, k, (mp + k) % M).wait_send()
        return total

    def drain(n):
        for p in range(R):
            zsend(n, p, wait=True)
            if n > 0:
                @pl.when(p != r)
                def _():
                    for k in range(1, M):
                        xcopy(n, p, k).wait_send()

    def first_pass():
        xg[r] = w_ref[...]
        zsend(0, r)
        part[...] = jnp.zeros_like(part)

        def outer(i, carry):
            p = piece_at(i)

            @pl.when(i > 0)
            def _():
                zwait(0, p)
                zsend(0, p)

            def inner(k, carry):
                first_block(i * C + k, p)
                return carry

            lax.fori_loop(0, C, inner, carry)

            @pl.when(i == 0)
            def _():
                for k in range(1, M):
                    diag_copy(mp, k, (mp + k) % M).start()

            return carry

        lax.fori_loop(0, R - 1, outer, 0)
        last = piece_at(R - 1)
        if R > 1:
            zwait(0, last)
            zsend(0, last)
        total = finish(0, lambda k, cc: first_block((R - 1) * C + k, last))
        drain(0)
        for k in range(1, M):
            other = (mp + M - k) % M
            diag_copy(other, k, other).wait_recv()
            diag_copy(mp, k, (mp + k) % M).wait_send()
        return total

    def later_pass(n):
        zsend(n, r)
        part[...] = jnp.zeros_like(part)

        def ready(p):
            for k in range(1, M):
                xwait(n, p, k)

        def outer(i, carry):
            p = piece_at(i)
            zwait(n, p)
            zsend(n, p)
            for k in range(1, M):
                xcopy(n, p, k).start()
            before = piece_at(i - 1)

            @pl.when(i > 1)
            def _():
                ready(before)

            def inner(cc, carry):
                later_block(n, cc, before)
                return carry

            return lax.fori_loop(0, C, inner, carry)

        lax.fori_loop(1, R, outer, 0)
        last = piece_at(R - 1)
        if R > 1:
            ready(last)
        total = finish(n, lambda k, cc: later_block(n, cc, last))
        drain(n)
        return total

    def reduce_small(it, value):
        sc1[it, c] = value
        for k in range(1, C):
            remote(sc1.at[it, c], sc1.at[it, c], s1s.at[it, k - 1], s1r.at[it, k - 1],
                   at_col((c + k) % C)).start()
        for k in range(1, C):
            other = (c + C - k) % C
            remote(sc1.at[it, other], sc1.at[it, other], s1s.at[it, k - 1], s1r.at[it, k - 1],
                   at_col(other)).wait_recv()
        sc2[it, r] = jnp.sum(sc1[it], axis=0)
        for k in range(1, R):
            remote(sc2.at[it, r], sc2.at[it, r], s2s.at[it, k - 1], s2r.at[it, k - 1],
                   at_row((r + k) % R)).start()
        for k in range(1, R):
            other = (r + R - k) % R
            remote(sc2.at[it, other], sc2.at[it, other], s2s.at[it, k - 1], s2r.at[it, k - 1],
                   at_row(other)).wait_recv()
        total = jnp.sum(sc2[it], axis=0)
        for k in range(1, C):
            remote(sc1.at[it, c], sc1.at[it, c], s1s.at[it, k - 1], s1r.at[it, k - 1],
                   at_col((c + k) % C)).wait_send()
        for k in range(1, R):
            remote(sc2.at[it, r], sc2.at[it, r], s2s.at[it, k - 1], s2r.at[it, k - 1],
                   at_row((r + k) % R)).wait_send()
        return total

    def dots(*pairs):
        sums = [jnp.sum(a * b, axis=0, keepdims=True) for a, b in pairs]
        sums.append(jnp.zeros((8 - len(pairs), width), F32))
        return jnp.concatenate(sums, axis=0)

    target = first_pass()
    resid[...] = target
    dirn[...] = target
    lg[0, r] = target.astype(BF16)
    norm_now = None
    for it in range(ITERS):
        applied = later_pass(it + 1)
        wide = lg[it, r].astype(F32)
        scale = damp[...] + diag[0]
        for m in range(1, n_mp):
            scale += diag[m]
        applied = applied + scale * wide
        old = resid[...]
        if it + 1 < ITERS:
            pairs = [(wide, applied), (old, applied), (applied, applied)]
            if norm_now is None:
                pairs.append((old, old))
            sums = reduce_small(it, dots(*pairs))
            if norm_now is None:
                norm_now = sums[3:4]
        else:
            sums = reduce_small(it, dots((wide, applied)))
        step = norm_now / sums[0:1]
        direction = dirn[...]
        if it == 0:
            merged[...] = step * direction
        else:
            merged[...] += step * direction
        new = old - step * applied
        resid[...] = new
        if it + 1 < ITERS:
            norm_next = norm_now + step * (step * sums[2:3] - 2.0 * sums[1:2])
            direction = new + (norm_next / norm_now) * direction
            dirn[...] = direction
            lg[it + 1, r] = direction.astype(BF16)
            norm_now = norm_next


def solution(mesh):
    n_mp, n_row, n_col = mesh.shape["mp"], mesh.shape["row"], mesh.shape["col"]

    def on_device(gram_tiles, weights, damping):
        shape = gram_tiles.shape
        models, piece, width = shape[0], weights.shape[1], weights.shape[2]
        passes, groups = ITERS + 1, n_col // 2
        gram = gram_tiles.reshape(models, shape[1], shape[3], shape[4])
        dma = pltpu.SemaphoreType.DMA
        vmem = pl.BlockSpec(memory_space=pltpu.VMEM)
        out = jax.ShapeDtypeStruct((piece, width), F32)
        return pl.pallas_call(
            functools.partial(kernel, n_mp, n_row, n_col),
            out_shape=(out, out),
            in_specs=[pl.BlockSpec(memory_space=pl.ANY), vmem, vmem],
            out_specs=(vmem, vmem),
            scratch_shapes=[
                pltpu.VMEM((n_col, n_row, piece, piece), BF16),
                pltpu.VMEM((NBUF, models, min(piece, 256), piece), BF16),
                pltpu.VMEM((n_col, piece, width), F32),
                pltpu.VMEM((n_row, models, piece, width), BF16),
                pltpu.VMEM((ITERS, n_row, piece, width), BF16),
                pltpu.VMEM((groups, piece, width), BF16),
                pltpu.VMEM((passes, groups, piece, width), BF16),
                pltpu.VMEM((groups, piece, width), BF16),
                pltpu.VMEM((passes, groups, piece, width), BF16),
                pltpu.VMEM((n_mp, piece, width), F32),
                pltpu.VMEM((ITERS, n_mp, piece, width), BF16),
                pltpu.VMEM((n_mp, piece, width), F32),
                pltpu.VMEM((piece, width), F32),
                pltpu.VMEM((ITERS, n_col, 8, width), F32),
                pltpu.VMEM((ITERS, n_row, 8, width), F32),
                dma((NBUF,)),
                dma((passes, 2, n_row)),
                dma((passes, n_row)),
                dma((passes, n_mp, n_row)),
                dma((passes, n_mp, n_row)),
                dma((passes, groups)),
                dma((passes, groups)),
                dma((passes, groups)),
                dma((passes, groups)),
                dma((passes, n_mp)),
                dma((passes, n_mp)),
                dma((n_mp,)),
                dma((n_mp,)),
                dma((ITERS, n_col)),
                dma((ITERS, n_col)),
                dma((ITERS, n_row)),
                dma((ITERS, n_row)),
            ],
            compiler_params=pltpu.CompilerParams(
                collective_id=0, has_side_effects=True, vmem_limit_bytes=62 * 1024 * 1024),
        )(gram, weights, damping.reshape(1, width))

    in_specs = (P("mp", None, "row", None, "col"), P("mp", ("col", "row"), None), P())
    out_specs = (P(("col", "row"), None), P(("col", "row"), None))
    return jax.shard_map(
        on_device, mesh=mesh, in_specs=in_specs, out_specs=out_specs, check_vma=False
    )
```

time: 492 us -> 172 us (0.35)
  waiting for transfers between devices: 289 us -> 0 us
  Pallas kernels: 0 us -> 168 us
  blocking collectives: 95.8 us -> 0 us
  matrix products: 81.5 us -> 0 us
  between operations: 13.9 us -> 0.64 us
  other arithmetic: 8.54 us -> 0 us
    pallas_call x0 -> x1, Pallas kernels: none -> 168 us  [on_device(): pl.pallas_call(functools.partial(kernel, n_mp, n_row, n_col), out_shape=(...]
    all_gather x3 -> x0, waiting for transfers between devices: 103 us -> none  [apply_models(): lax.all_gather(vectors, 'row', axis=1, tiled=True)]
    psum x3 -> x0, blocking collectives: 95.8 us -> none  [the longest x2 62.6 us: squares(): return lax.psum(jnp.sum(residual * residual, axis=0), ('row', 'col'))]
    psum x3 -> x0, waiting for transfers between devices: 92.7 us -> none  [apply_models(): return (lax.psum(summed, 'mp'), partial_value)]
    reduce_scatter x3 -> x0, waiting for transfers between devices: 92.3 us -> none  [apply_models(): lax.psum_scatter(partial_value, 'col', scatter_dimension=0, tiled=True)]
    dot_general x3 -> x0, matrix products: 81.5 us -> none  [contract_rows(): jnp.einsum('mij,mjk->ik', gram_tile, spread, preferred_element_type=jnp.f...]
  transfers between devices with their start and end apart: 9 -> 0, of which waited for: 9 -> 0; matrix products, arithmetic and copies ran while one was open for 0% -> 0% of each run, Pallas kernels for 0% -> 0%
where the time goes in v1:
time: 172 us
  Pallas kernels  168 us (98%)
  local copies, waits for them, and re-layouts  3.74 us (2%)
    pallas_call x1, Pallas kernels, on_device(): pl.pallas_call(functools.partial(kernel, n_mp, n_row, n_col), out_shape=(...  168 us
    unnamed x2, local copies, waits for them, and re-layouts  3.74 us

profile of v1, /device:TPU:0, one launch (start us, length us, event | category | flops | bytes accessed | tf_op | source)
XLA Modules:
  0.0 171.9 jit_solution(2727011781669015649)
XLA Ops:
  0.6 167.6 %shard_map.50 = (f32[1024,128]{1,0:T(8,128)}, f32[1024,128]{1,0:T(8,128)}) custom-call(bf16[2,4,1024,4096]{3,2,1,0:T(8,128)(2,1)} %bitcast.gram, bf16[2,1024,128]{2,1,0:T(8,128)(2,1)} %w_ref.1, f32[1,128]{1,0:T(1,128)} %bitcast.2), custom_call_target="tpu_custom_call" | custom-call | tf_op jit(solution)/shard_map/pallas_call | solution.py:373
  168.2 1.9 %copy.7 = f32[1024,128]{1,0:T(8,128)} copy(f32[1024,128]{1,0:T(8,128)} %get-tuple-element.4) | data formatting | bytes 1048576
  170.1 1.9 %copy.8 = f32[1024,128]{1,0:T(8,128)} copy(f32[1024,128]{1,0:T(8,128)} %get-tuple-element.5) | data formatting | bytes 1048576
